TPU v7x, 32 devices: a whole 2x2x4 slice. The times are simulated.
32 devices in a mesh: dp: 4 (over z), ctx: 2 (over x), tensor: 4 (over y, core).
Axes of the slice: x: 2, y: 2, z: 4, core: 2. Of those that a mesh axis runs over, the one named last changes fastest.
Arguments:
- inputs: bfloat16 [4, 1024, 768], P('dp', 'ctx'), may hold values from -6 to 6
- gain_attention: float32 [768], replicated, may hold values from 0.5 to 1.5
- w_query: bfloat16 [768, 768], P(('dp', 'ctx'), 'tensor'), may hold values from -0.21875 to 0.21875
- w_key: bfloat16 [768, 768], P(('dp', 'ctx'), 'tensor'), may hold values from -0.21875 to 0.21875
- w_value: bfloat16 [768, 768], P(('dp', 'ctx'), 'tensor'), may hold values from -0.21875 to 0.21875
- w_output: bfloat16 [768, 768], P(('dp', 'ctx'), 'tensor'), may hold values from -1.5 to 1.5
- bias_table: float32 [32, 12], P(None, 'tensor'), may hold values from -4 to 4
- bucket_start: int32 [32], replicated, may hold values from 0 to 1023, as said below
- gain_experts: float32 [768], replicated, may hold values from 0.5 to 1.5
- w_router: bfloat16 [768, 8], replicated, may hold values from -0.15625 to 0.15625
- w_up: bfloat16 [8, 768, 3072], P(('dp', 'ctx'), None, 'tensor'), may hold values from -0.21875 to 0.21875
- w_down: bfloat16 [8, 3072, 768], P(('dp', 'ctx'), 'tensor'), may hold values from -0.15625 to 0.15625
- expert_ids: int32 [4, 1024, 2], P('dp', 'ctx'), may hold values from 0 to 7, as said below
- slot_index: int32 [4, 1024, 2], P('dp', 'ctx'), may hold values from -1 to 159, as said below
- cotangent: bfloat16 [4, 1024, 768], P('dp', 'ctx'), may hold values from -6 to 6
Outputs:
- layer_out: bfloat16 [4, 1024, 768], P('dp', 'ctx')
- grad_inputs: float32 [4, 1024, 768], P('dp', 'ctx')
- grad_gain_attention: float32 [768], replicated
- grad_w_query: float32 [768, 768], P(None, 'tensor')
- grad_w_key: float32 [768, 768], P(None, 'tensor')
- grad_w_value: float32 [768, 768], P(None, 'tensor')
- grad_w_output: float32 [768, 768], P(None, 'tensor')
- grad_bias_table: float32 [32, 12], P(None, 'tensor')
- grad_gain_experts: float32 [768], replicated
- grad_router: float32 [768, 8], replicated
- grad_w_up: float32 [8, 768, 3072], P(('dp', 'ctx'), None, 'tensor')
- grad_w_down: float32 [8, 3072, 768], P(('dp', 'ctx'), 'tensor')
Inputs may be any that keep to these rules, and one draw needn't show every extreme that they name: `expert_ids`: each token names 2 different experts. `slot_index`: take the 512 tokens of one index of dp and ctx by sequence, then position, then choice. The choices of these tokens that name one expert get slots 0, 1, 2 and so on in that order; those past 160 get -1. In every draw some expert gets all 160 slots from every index of dp and ctx. bucket_start[b] = b for b <= 16, strictly increasing after that, and bucket_start[31] = 1023.
All inputs are finite; a program needn't handle non-finite values.
Results may differ from a plain program's by a relative error of at most 0.017.
Values may be sent and summed in bfloat16 or wider, within the bound.
A program may use at most 128 MiB of HBM per device.

v0:
```python
import jax
import jax.numpy as jnp
from jax import lax
from jax.sharding import PartitionSpec as P

EPS = 1e-06
MASKED = -1e30
HIGHEST = lax.Precision.HIGHEST


def toeplitz(diagonals, height, breadth):
    heads, span = diagonals.shape
    padded = jnp.concatenate([diagonals, jnp.zeros((heads, 1), diagonals.dtype)], axis=1)
    tiled = jnp.broadcast_to(padded[:, None, :], (heads, height, span + 1)).reshape(
        heads, height * (span + 1)
    )
    skewed = tiled[:, : height * span].reshape(heads, height, span)
    return skewed[:, :, height - 1 : height - 1 + breadth]


def diagonal_sums(values, height, breadth):
    heads = values.shape[0]
    span = height + breadth - 1
    placed = jnp.pad(values, ((0, 0), (0, 0), (height - 1, 0))).reshape(heads, height * span)
    skewed = jnp.pad(placed, ((0, 0), (0, height))).reshape(heads, height, span + 1)
    return jnp.sum(skewed, axis=1, dtype=jnp.float32)[:, :span]


def distance_table(starts, offset, height, breadth):
    span = height + breadth - 1
    distance = offset + height - 1 - jnp.arange(span, dtype=jnp.int32)
    bucket = jnp.sum((distance[:, None] >= starts[None, :]).astype(jnp.int32), axis=1) - 1
    levels = jnp.arange(starts.shape[0], dtype=jnp.int32)
    return ((bucket[:, None] == levels[None, :]) & (distance[:, None] >= 0)).astype(jnp.float32)


def masked_logits(query, keys, bias_table, starts, first_query, first_key):
    height = query.shape[0]
    breadth = keys.shape[0]
    table = distance_table(starts, first_query - first_key, height, breadth)
    diagonals = jnp.dot(table, bias_table, precision=HIGHEST).T
    raw = jnp.einsum("qhd,khd->hqk", query, keys, preferred_element_type=jnp.float32)
    logits = raw * query.shape[2] ** (-0.5) + toeplitz(diagonals, height, breadth)
    query_pos = first_query + jnp.arange(height, dtype=jnp.int32)
    key_pos = first_key + jnp.arange(breadth, dtype=jnp.int32)
    causal = key_pos[None, :] <= query_pos[:, None]
    return (jnp.where(causal[None], logits, MASKED), table)


def softmax_grads(
    query, keys, values, grad_mixed, log_total, bias_table, starts, first_query, first_key
):
    masked, table = masked_logits(query, keys, bias_table, starts, first_query, first_key)
    shares = jnp.exp(masked - log_total[:, :, None])
    grad_shares = jnp.einsum("qhd,khd->hqk", grad_mixed, values, preferred_element_type=jnp.float32)
    return (shares, grad_shares, table)


def norm_forward(value, gain):
    scale = lax.rsqrt(jnp.mean(value * value, axis=-1, keepdims=True) + EPS)
    return (value * scale * gain, scale)


def norm_backward(value, scale, gain, grad_normed):
    scaled = grad_normed * gain
    grad_value = scale * scaled - value * scale**3 * jnp.mean(
        value * scaled, axis=-1, keepdims=True
    )
    return (grad_value, jnp.sum(grad_normed * value * scale, axis=0))


def on_device(
    inputs,
    gain_attention,
    w_query,
    w_key,
    w_value,
    w_output,
    bias_table,
    bucket_start,
    gain_experts,
    w_router,
    w_up,
    w_down,
    expert_ids,
    slot_index,
    cotangent,
):
    sequences, rows, width = inputs.shape
    tokens = sequences * rows
    experts = w_router.shape[1]
    top_count = expert_ids.shape[2]
    capacity = 5 * tokens * top_count // (4 * experts)
    heads_local = bias_table.shape[1]
    first_query = lax.axis_index("ctx") * rows
    reached = lax.axis_index("ctx") + 1
    source = inputs.astype(jnp.float32).reshape(tokens, width)
    normed_one, scale_one = norm_forward(source, gain_attention)
    normed_one = normed_one.astype(jnp.bfloat16)
    query_w, key_w, value_w, output_w = (
        lax.all_gather(w_query, ("dp", "ctx"), axis=0, tiled=True),
        lax.all_gather(w_key, ("dp", "ctx"), axis=0, tiled=True),
        lax.all_gather(w_value, ("dp", "ctx"), axis=0, tiled=True),
        lax.all_gather(w_output, ("dp", "ctx"), axis=0, tiled=True),
    )
    head_dim = query_w.shape[1] // heads_local
    scale = head_dim ** (-0.5)

    def project(weight):
        return (
            jnp.dot(normed_one, weight, preferred_element_type=jnp.float32)
            .astype(jnp.bfloat16)
            .reshape(sequences, rows, heads_local * head_dim)
        )

    query_flat = project(query_w)
    keys_all, values_all = (
        lax.all_gather(project(key_w), "ctx", axis=1, tiled=True),
        lax.all_gather(project(value_w), "ctx", axis=1, tiled=True),
    )
    length = keys_all.shape[1]
    query = query_flat.reshape(sequences, rows, heads_local, head_dim)
    keys_all = keys_all.reshape(sequences, length, heads_local, head_dim)
    values_all = values_all.reshape(sequences, length, heads_local, head_dim)

    def block_of(whole, step):
        return lax.dynamic_slice_in_dim(whole, step * rows, rows, 0)

    def attend(pieces):
        one_query, one_keys, one_values = pieces

        def total_step(step, carry):
            peak, total = carry
            masked, _ = masked_logits(
                one_query,
                block_of(one_keys, step),
                bias_table,
                bucket_start,
                first_query,
                step * rows,
            )
            new_peak = jnp.maximum(peak, jnp.max(masked, axis=-1))
            total = total * jnp.exp(peak - new_peak) + jnp.sum(
                jnp.exp(masked - new_peak[..., None]), axis=-1
            )
            return (new_peak, total)

        begin = (
            jnp.full((heads_local, rows), MASKED, jnp.float32),
            jnp.zeros((heads_local, rows), jnp.float32),
        )
        peak, total = lax.fori_loop(0, reached, total_step, begin)
        log_total = peak + jnp.log(total)

        def mix_step(step, acc):
            masked, _ = masked_logits(
                one_query,
                block_of(one_keys, step),
                bias_table,
                bucket_start,
                first_query,
                step * rows,
            )
            shares = jnp.exp(masked - log_total[..., None]).astype(jnp.bfloat16)
            return acc + jnp.einsum(
                "hqk,khd->qhd",
                shares,
                block_of(one_values, step),
                preferred_element_type=jnp.float32,
            )

        mixed = lax.fori_loop(
            0, reached, mix_step, jnp.zeros((rows, heads_local, head_dim), jnp.float32)
        )
        return (mixed.astype(jnp.bfloat16), log_total)

    mixed, log_total = lax.map(attend, (query, keys_all, values_all))
    attended_rows = mixed.reshape(tokens, heads_local * head_dim)
    branch = lax.dot_general(
        attended_rows, output_w, (((1,), (1,)), ((), ())), preferred_element_type=jnp.float32
    )
    hidden_one = source + lax.psum(branch, "tensor")
    normed_two, scale_two = norm_forward(hidden_one, gain_experts)
    normed_two = normed_two.astype(jnp.bfloat16)
    router_logits = jnp.dot(normed_two, w_router, preferred_element_type=jnp.float32)
    route = expert_ids.reshape(tokens, top_count)
    place = slot_index.reshape(tokens, top_count)
    picks = route[:, :, None] == jnp.arange(experts, dtype=jnp.int32)[None, None, :]
    chosen = jnp.sum(jnp.where(picks, router_logits[:, None, :], 0.0), axis=-1)
    gates = jax.nn.softmax(chosen, axis=-1)
    kept = place >= 0
    target = jnp.where(kept, route * capacity + place, experts * capacity).reshape(-1)
    safe_target = jnp.minimum(target, experts * capacity - 1)
    outgoing = (
        jnp.zeros((experts * capacity, width), jnp.bfloat16)
        .at[target]
        .set(jnp.repeat(normed_two, top_count, axis=0), mode="drop")
        .reshape(experts, capacity, width)
    )
    up_weight = w_up[0]
    down_weight = w_down[0]
    buffer = lax.all_to_all(outgoing, ("dp", "ctx"), split_axis=0, concat_axis=0, tiled=True)
    before = jnp.einsum("scd,df->scf", buffer, up_weight, preferred_element_type=jnp.float32)
    activated, gelu_pullback = jax.vjp(jax.nn.gelu, before)
    activated = activated.astype(jnp.bfloat16)
    partial_out = jnp.einsum(
        "scf,fd->scd", activated, down_weight, preferred_element_type=jnp.float32
    )
    produced = lax.psum(partial_out, "tensor").astype(jnp.bfloat16)
    returned = lax.all_to_all(
        produced, ("dp", "ctx"), split_axis=0, concat_axis=0, tiled=True
    ).reshape(experts * capacity, width)
    mask_rows = kept.reshape(tokens, top_count, 1)
    picked = jnp.where(
        mask_rows,
        jnp.take(returned, safe_target, axis=0)
        .reshape(tokens, top_count, width)
        .astype(jnp.float32),
        0.0,
    )
    result = hidden_one + jnp.sum(gates[:, :, None] * picked, axis=1)
    grad_result = cotangent.astype(jnp.float32).reshape(tokens, width)
    grad_gates = jnp.sum(grad_result[:, None, :] * picked, axis=-1)
    grad_rows = (
        (gates[:, :, None] * grad_result[:, None, :])
        .astype(jnp.bfloat16)
        .reshape(tokens * top_count, width)
    )
    back_out = (
        jnp.zeros((experts * capacity, width), jnp.bfloat16)
        .at[target]
        .set(grad_rows, mode="drop")
        .reshape(experts, capacity, width)
    )
    grad_produced = lax.all_to_all(back_out, ("dp", "ctx"), split_axis=0, concat_axis=0, tiled=True)
    grad_down = jnp.einsum(
        "scf,scd->fd", activated, grad_produced, preferred_element_type=jnp.float32
    )
    grad_active = jnp.einsum(
        "scd,fd->scf", grad_produced, down_weight, preferred_element_type=jnp.float32
    )
    grad_before = gelu_pullback(grad_active)[0].astype(jnp.bfloat16)
    grad_up = jnp.einsum("scd,scf->df", buffer, grad_before, preferred_element_type=jnp.float32)
    grad_arrived = jnp.einsum(
        "scf,df->scd", grad_before, up_weight, preferred_element_type=jnp.float32
    )
    grad_sent = (
        lax.all_to_all(
            grad_arrived.astype(jnp.bfloat16),
            ("dp", "ctx"),
            split_axis=0,
            concat_axis=0,
            tiled=True,
        )
        .astype(grad_arrived.dtype)
        .reshape(experts * capacity, width)
    )
    dispatch_part = jnp.sum(
        jnp.where(
            mask_rows,
            jnp.take(grad_sent, safe_target, axis=0).reshape(tokens, top_count, width),
            0.0,
        ),
        axis=1,
    )
    grad_normed_two = lax.psum(dispatch_part.astype(jnp.bfloat16), "tensor").astype(jnp.float32)
    inner_gate = jnp.sum(gates * grad_gates, axis=-1, keepdims=True)
    grad_chosen = gates * (grad_gates - inner_gate)
    grad_logits_router = jnp.sum(jnp.where(picks, grad_chosen[:, :, None], 0.0), axis=1).astype(
        jnp.bfloat16
    )
    grad_router = lax.dot_general(
        normed_two, grad_logits_router, (((0,), (0,)), ((), ())), preferred_element_type=jnp.float32
    )
    grad_normed_two = grad_normed_two + lax.dot_general(
        grad_logits_router, w_router, (((1,), (1,)), ((), ())), preferred_element_type=jnp.float32
    )
    grad_hidden_back, grad_gain_two = norm_backward(
        hidden_one, scale_two, gain_experts, grad_normed_two
    )
    grad_hidden_one = grad_result + grad_hidden_back
    grad_branch = grad_hidden_one.astype(jnp.bfloat16)
    grad_mixed = jnp.dot(grad_branch, output_w, preferred_element_type=jnp.float32).astype(
        jnp.bfloat16
    )
    grad_output_w = lax.dot_general(
        grad_branch, attended_rows, (((0,), (0,)), ((), ())), preferred_element_type=jnp.float32
    )
    grad_mixed_heads = grad_mixed.reshape(sequences, rows, heads_local, head_dim)
    buckets = bias_table.shape[0]

    def query_pass(one_query, one_keys, one_values, one_grad, one_log):

        def inner_step(step, acc):
            shares, grad_shares, _ = softmax_grads(
                one_query,
                block_of(one_keys, step),
                block_of(one_values, step),
                one_grad,
                one_log,
                bias_table,
                bucket_start,
                first_query,
                step * rows,
            )
            return acc + jnp.sum(shares * grad_shares, axis=-1)

        inner = lax.fori_loop(0, reached, inner_step, jnp.zeros((heads_local, rows), jnp.float32))

        def grad_step(step, carry):
            keys_block = block_of(one_keys, step)
            shares, grad_shares, table = softmax_grads(
                one_query,
                keys_block,
                block_of(one_values, step),
                one_grad,
                one_log,
                bias_table,
                bucket_start,
                first_query,
                step * rows,
            )
            grad_logits = (shares * (grad_shares - inner[..., None])).astype(jnp.bfloat16)
            query_acc = (
                carry[0]
                + jnp.einsum(
                    "hqk,khd->qhd", grad_logits, keys_block, preferred_element_type=jnp.float32
                )
                * scale
            )
            sums = diagonal_sums(grad_logits, rows, rows)
            table_acc = carry[1] + jnp.dot(table.T, sums.T, precision=HIGHEST)
            keys_piece = (
                jnp.einsum(
                    "hqk,qhd->khd", grad_logits, one_query, preferred_element_type=jnp.float32
                )
                * scale
            )
            values_piece = jnp.einsum(
                "hqk,qhd->khd",
                shares.astype(jnp.bfloat16),
                one_grad,
                preferred_element_type=jnp.float32,
            )
            keys_acc = lax.dynamic_update_slice_in_dim(carry[2], keys_piece, step * rows, 0)
            values_acc = lax.dynamic_update_slice_in_dim(carry[3], values_piece, step * rows, 0)
            return (query_acc, table_acc, keys_acc, values_acc)

        begin = (
            jnp.zeros((rows, heads_local, head_dim), jnp.float32),
            jnp.zeros((buckets, heads_local), jnp.float32),
        )
        whole = jnp.zeros((length, heads_local, head_dim), jnp.float32)
        begin = begin + (whole, whole)
        return (lax.fori_loop(0, reached, grad_step, begin), inner)

    def whole_side(pieces):
        one_query, one_keys, one_values, one_grad, one_log = pieces
        sums, _ = query_pass(one_query, one_keys, one_values, one_grad, one_log)
        return sums

    grad_query, grad_tables, keys_part, values_part = lax.map(
        whole_side, (query, keys_all, values_all, grad_mixed_heads, log_total)
    )
    grad_keys, grad_values = (
        lax.psum_scatter(
            keys_part.reshape(sequences, length, heads_local * head_dim).astype(jnp.bfloat16),
            "ctx",
            scatter_dimension=1,
            tiled=True,
        ).astype(jnp.float32),
        lax.psum_scatter(
            values_part.reshape(sequences, length, heads_local * head_dim).astype(jnp.bfloat16),
            "ctx",
            scatter_dimension=1,
            tiled=True,
        ).astype(jnp.float32),
    )
    grad_table = jnp.sum(grad_tables, axis=0)
    query_grad = grad_query.reshape(tokens, heads_local * head_dim).astype(jnp.bfloat16)
    key_grad = grad_keys.reshape(tokens, heads_local * head_dim).astype(jnp.bfloat16)
    value_grad = grad_values.reshape(tokens, heads_local * head_dim).astype(jnp.bfloat16)

    def pull(grad_part, weight):
        return lax.dot_general(
            grad_part, weight, (((1,), (1,)), ((), ())), preferred_element_type=jnp.float32
        )

    def weight_grad(grad_part):
        return lax.dot_general(
            normed_one, grad_part, (((0,), (0,)), ((), ())), preferred_element_type=jnp.float32
        )

    grad_normed_one = lax.psum(
        (pull(query_grad, query_w) + pull(key_grad, key_w) + pull(value_grad, value_w)).astype(
            jnp.bfloat16
        ),
        "tensor",
    ).astype(jnp.float32)
    grad_source_back, grad_gain_one = norm_backward(
        source, scale_one, gain_attention, grad_normed_one
    )
    grad_source = grad_hidden_one + grad_source_back
    summed = lax.psum(
        (
            grad_gain_one,
            grad_gain_two,
            grad_router,
            grad_table,
            weight_grad(query_grad),
            weight_grad(key_grad),
            weight_grad(value_grad),
            grad_output_w,
        ),
        ("dp", "ctx"),
    )
    return (
        result.astype(jnp.bfloat16).reshape(sequences, rows, width),
        grad_source.reshape(sequences, rows, width),
        summed[0],
        summed[4],
        summed[5],
        summed[6],
        summed[7],
        summed[3],
        summed[1],
        summed[2],
        grad_up[None],
        grad_down[None],
    )


def solution(mesh):
    in_specs = (
        P("dp", "ctx", None),
        P(),
        P(("dp", "ctx"), "tensor"),
        P(("dp", "ctx"), "tensor"),
        P(("dp", "ctx"), "tensor"),
        P(("dp", "ctx"), "tensor"),
        P(None, "tensor"),
        P(),
        P(),
        P(),
        P(("dp", "ctx"), None, "tensor"),
        P(("dp", "ctx"), "tensor", None),
        P("dp", "ctx", None),
        P("dp", "ctx", None),
        P("dp", "ctx", None),
    )
    out_specs = (
        P("dp", "ctx", None),
        P("dp", "ctx", None),
        P(),
        P(None, "tensor"),
        P(None, "tensor"),
        P(None, "tensor"),
        P(None, "tensor"),
        P(None, "tensor"),
        P(),
        P(),
        P(("dp", "ctx"), None, "tensor"),
        P(("dp", "ctx"), "tensor", None),
    )
    return jax.shard_map(
        on_device, mesh=mesh, in_specs=in_specs, out_specs=out_specs, check_vma=False
    )
```

profile of v0, /device:TPU:0, one launch (start us, length us, event | category | flops | bytes accessed | tf_op | source)
XLA Modules:
  0.0 1201.1 jit_solution(4376643864783591724)
XLA Ops:
  9.4 32.9 %all_gather.22 = bf16[768,192]{1,0:T(8,128)(2,1)S(1)} all-gather(bf16[96,192]{1,0:T(8,128)(2,1)} %param.25), channel_id=1, replica_groups=mesh['dp'=4,'ctx'=2,'tensor'=4] {'dp','ctx'}, dimensions={0}, use_global_device_ids=true | all-gather | bytes 331776 | tf_op jit(solution)/shard_map/all_gather | solution.py:101
  42.3 31.3 %all_gather.20 = bf16[768,192]{1,0:T(8,128)(2,1)S(1)} all-gather(bf16[96,192]{1,0:T(8,128)(2,1)} %param.26), channel_id=1, replica_groups=mesh['dp'=4,'ctx'=2,'tensor'=4] {'dp','ctx'}, dimensions={0}, use_global_device_ids=true | all-gather | bytes 331776 | tf_op jit(solution)/shard_map/all_gather | solution.py:102
  76.0 6.5 all-gather.1
  82.5 41.5 %while.96 = (s32[]{:T(128)}, f32[3,512]{1,0:T(4,128)S(1)}, f32[3,512]{1,0:T(4,128)S(1)}, s32[]{:T(128)}, s32[]{:T(128)}, /*index=5*/bf16[1024,3,64]{0,2,1:T(8,12...) while((s32[]{:T(128)}, f32[3,512]{1,0:T(4,128)S(1)}, ...), condition=%wide.region_5.6_spmd, body=%wide.region_1.5_spmd.sunk | while | flops 106993376 | bytes 69739248 | solution.py:152
  84.1 3.5 broadcast_bitcast_fusion.8
  87.6 7.1 copy.112
  94.7 4.1 slice.114
  98.8 13.2 %reshape.802 = f32[3,512,1023]{2,1,0:T(8,128)} reshape(f32[3,523776]{1,0:T(4,128)} %slice.114) | data formatting | bytes 12570624 | tf_op jit(solution)/shard_map/while/body/eval_jaxpr/while/body/reshape | solution.py:17
  112.0 4.6 slice.115
  116.7 3.6 copy.113
  123.9 72.1 %all_gather.18 = bf16[768,192]{1,0:T(8,128)(2,1)S(1)} all-gather(bf16[96,192]{1,0:T(8,128)(2,1)S(1)} %copy-done.53), channel_id=1, replica_groups=mesh['dp'=4,'ctx'=2,'tensor'=4] {'dp','ctx'}, dimensions={0}, use_global_device_ids=true | all-gather | bytes 331776 | tf_op jit(solution)/shard_map/all_gather | solution.py:103
  198.4 7.0 all-gather
  205.4 33.0 %all_gather.23 = bf16[768,192]{1,0:T(8,128)(2,1)} all-gather(bf16[96,192]{1,0:T(8,128)(2,1)S(1)} %copy-done.54), channel_id=1, replica_groups=mesh['dp'=4,'ctx'=2,'tensor'=4] {'dp','ctx'}, dimensions={0}, use_global_device_ids=true | all-gather | bytes 331776 | tf_op jit(solution)/shard_map/all_gather | solution.py:104
  239.2 42.1 %while.97 = (s32[]{:T(128)}, f32[512,3,64]{0,2,1:T(8,128)}, s32[]{:T(128)}, bf16[1024,3,64]{0,2,1:T(8,128)(2,1)}, s32[]{:T(128)}, /*index=5*/bf16[1024,3,64]{0,2...) while((s32[]{:T(128)}, f32[512,3,64]{0,2,1:T(8,128)}, ...), condition=%wide.region_8.9_spmd, body=%wide.region_6.8_spmd.sunk | while | flops 206965472 | bytes 69078848 | solution.py:172
  240.8 3.5 broadcast_bitcast_fusion.9
  244.3 7.1 copy.114
  251.4 4.1 slice.116
  255.5 13.2 %reshape.803 = f32[3,512,1023]{2,1,0:T(8,128)} reshape(f32[3,523776]{1,0:T(4,128)} %slice.116) | data formatting | bytes 12570624 | tf_op jit(solution)/shard_map/while/body/eval_jaxpr/while/body/reshape | solution.py:17
  268.7 4.6 slice.117
  273.4 3.7 copy.115
  285.4 85.8 %all-reduce.14.cloned.1.call-done = f32[512,768]{1,0:T(8,128)} async-done(((f32[512,768]{1,0:T(8,128)}), f32[512,768]{1,0:T(8,128)}) %all-reduce.14.cloned.1.call-update) | async-done | bytes 1572880 | tf_op jit(solution)/shard_map/psum | solution.py:182
  377.4 6.4 scatter_custom_fusion
  383.8 51.1 %all_to_all.20 = bf16[8,160,768]{2,1,0:T(8,128)(2,1)S(1)} all-to-all(bf16[8,160,768]{2,1,0:T(8,128)(2,1)S(1)} %bitcast.315), channel_id=1, replica_groups=mesh['dp'=4,'ctx'=2,'tensor'=4] {'dp','ctx'}, dimensions={0} | all-to-all | bytes 3932160 | tf_op jit(solution)/shard_map/all_to_all | solution.py:202
  439.8 4.4 fusion.96
  444.2 71.9 %all-reduce.21 = bf16[8,160,768]{2,1,0:T(8,128)(2,1)} all-reduce(f32[8,160,768]{2,1,0:T(8,128)} %fusion.96), channel_id=1, replica_groups=mesh['dp'=4,'ctx'=2,'tensor'=4] {'tensor'}, use_global_device_ids=true, to_apply=%region_15.16 | all-reduce | flops 983040 | bytes 5898240 | tf_op jit(solution)/shard_map/psum | solution.py:209
  516.0 4.0 all-to-all-start.1
  524.8 5.3 mul.430
  531.7 34.8 %all-to-all-done.1 = bf16[8,160,768]{2,1,0:T(8,128)(2,1)S(1)} async-done(((bf16[8,160,768]{2,1,0:T(8,128)(2,1)}), bf16[8,160,768]{2,1,0:T(8,128)(2,1)S(1)}, u32[]{:S(2)}, u32[]{:S(2)}) %all-to-all-start.1) | async-done | bytes 1966112 | tf_op jit(solution)/shard_map/all_to_all | solution.py:210
  566.4 5.2 gather_fusion
  575.9 7.0 scatter_custom_fusion.1
  582.9 49.7 %all_to_all.21 = bf16[8,160,768]{2,1,0:T(8,128)(2,1)S(1)} all-to-all(bf16[8,160,768]{2,1,0:T(8,128)(2,1)S(1)} %bitcast.314), channel_id=1, replica_groups=mesh['dp'=4,'ctx'=2,'tensor'=4] {'dp','ctx'}, dimensions={0} | all-to-all | bytes 3932160 | tf_op jit(solution)/shard_map/all_to_all | solution.py:235
  632.6 3.7 fusion.74
  640.6 4.5 all-to-all-start.3
  646.6 42.7 %all-to-all-done.3 = bf16[8,160,768]{2,1,0:T(8,128)(2,1)} async-done(((bf16[8,160,768]{2,1,0:T(8,128)(2,1)}), bf16[8,160,768]{2,1,0:T(8,128)(2,1)}, u32[]{:S(2)}, u32[]{:S(2)}) %all-to-all-start.3) | async-done | bytes 1966112 | tf_op jit(solution)/shard_map/all_to_all | solution.py:248
  689.3 3.7 bitcast_convert_fusion
  693.0 8.0 gather_fusion.1
  701.0 5.2 gather.15
  706.2 12.9 %select_reduce_fusion = (bf16[512,768]{1,0:T(8,128)(2,1)}, f32[512,768]{1,0:T(8,128)}) fusion(f32[512,2,768]{2,1,0:T(2,128)} %gather.15, pred[512,2]{1,0:T(8,128)(4,1)S(1)} %copy.80, pred[512,2]{1,0:T(8,128)(4,1)S(1)} %copy.79, bf16[512,2,768]{2,1,0:T(2,128)(2,1)} %gather.13, f32[512,2]{1,0:T(8,128)S(1)} %copy-done.28), kind=kLoop, calls=%fused_computation.125 | loop fusion | flops 5505024 | bytes 7084032 | tf_op jit(solution)/shard_map/reduce_sum | solution.py:258
  719.2 32.8 %all-reduce.16.cloned.1.call-done = bf16[512,768]{1,0:T(8,128)(2,1)} async-done(((bf16[512,768]{1,0:T(8,128)(2,1)}), bf16[512,768]{1,0:T(8,128)(2,1)}) %all-reduce.16.cloned.1.call-update) | async-done | bytes 786448 | tf_op jit(solution)/shard_map/psum | solution.py:266
  757.6 43.7 %while.98 = (s32[]{:T(128)}, f32[3,512]{1,0:T(4,128)S(1)}, s32[]{:T(128)}, s32[]{:T(128)}, bf16[1024,3,64]{0,2,1:T(8,128)(2,1)S(1)}, /*index=5*/bf16[512,3,64]{0...) while((s32[]{:T(128)}, f32[3,512]{1,0:T(4,128)S(1)}, ...), condition=%wide.region_27.28_spmd, body=%wide.region_24.27_spmd.sunk | while | flops 207653600 | bytes 69036768 | solution.py:308
  764.6 7.1 copy.116
  771.7 4.1 slice.118
  775.7 13.2 %reshape.804 = f32[3,512,1023]{2,1,0:T(8,128)} reshape(f32[3,523776]{1,0:T(4,128)} %slice.118) | data formatting | bytes 12570624 | tf_op jit(solution)/shard_map/while/body/eval_jaxpr/while/body/reshape | solution.py:17
  789.0 4.6 slice.119
  793.6 3.6 copy.117
  797.2 4.0 fusion.229
  803.7 88.5 %while.99 = (s32[]{:T(128)}, f32[512,3,64]{0,2,1:T(8,128)}, f32[32,3]{0,1:T(4,128)S(1)}, bf16[1024,3,64]{0,2,1:T(8,128)(2,1)}, bf16[1024,3,64]{0,2,1:T(8,128)(2,...) while((s32[]{:T(128)}, f32[512,3,64]{0,2,1:T(8,128)}, ...), condition=%wide.region_31.32_spmd, body=%wide.region_28.31_spmd.sunk | while | flops 515897984 | bytes 124672688 | solution.py:355
  823.0 3.5 broadcast_bitcast_fusion.11
  826.4 7.1 copy.119
  833.5 4.1 slice.121
  837.6 13.2 %reshape.805 = f32[3,512,1023]{2,1,0:T(8,128)} reshape(f32[3,523776]{1,0:T(4,128)} %slice.121) | data formatting | bytes 12570624 | tf_op jit(solution)/shard_map/while/body/eval_jaxpr/while/body/reshape | solution.py:17
  850.8 4.6 slice.122
  855.5 3.6 copy.120
  867.5 4.2 pad.52.clone.2
  871.7 7.0 reshape.806
  878.7 5.5 reshape.807
  884.2 3.9 pad_convert_fusion.2
  898.6 120.4 %reduce-scatter.3.cloned.1.call-done = bf16[1,512,192]{1,2,0:T(8,128)(2,1)} async-done(((bf16[1,1024,192]{1,2,0:T(8,128)(2,1)}), bf16[1,512,192]{1,2,0:T(8,128)(2,1)}) %reduce-scatter.3.cloned.1.call-update) | async-done | bytes 196624 | tf_op jit(solution)/shard_map/reduce_scatter | solution.py:366
  1021.4 13.4 %reduce-scatter.5.cloned.1.call-done = bf16[1,512,192]{1,2,0:T(8,128)(2,1)} async-done(((bf16[1,1024,192]{1,2,0:T(8,128)(2,1)}), bf16[1,512,192]{1,2,0:T(8,128)(2,1)}) %reduce-scatter.5.cloned.1.call-update) | async-done | bytes 196624 | tf_op jit(solution)/shard_map/reduce_scatter | solution.py:372
  1041.0 5.5 convolution_bitcast_fusion.5
  1046.5 3.5 convolution_bitcast_fusion.4
  1050.0 23.0 %all-reduce.18.cloned.1.call-done = bf16[512,768]{1,0:T(8,128)(2,1)} async-done(((bf16[512,768]{1,0:T(8,128)(2,1)}), bf16[512,768]{1,0:T(8,128)(2,1)}) %all-reduce.18.cloned.1.call-update) | async-done | bytes 786448 | tf_op jit(solution)/shard_map/psum | solution.py:394
  1074.9 39.8 %all-reduce.6 = (f32[768]{0:T(1024)}, f32[32,3]{0,1:T(4,128)}, f32[768]{0:T(1024)}, f32[768,8]{0,1:T(8,128)}) all-reduce(f32[768]{0:T(1024)S(1)} %get-tuple-element.1146, f32[32,3]{0,1:T(4,128)S(1)} %get-tuple-element.1123, f32[768]{0:T(1024)S(1)} %copy-done.62, ...), channel_id=1, replica_groups=mesh['dp'=4,'ctx'=2,'tensor'=4] {'dp','ctx'}, use_global_device_ids=true, to_apply=%region_37.38 | all-reduce | flops 7776 | bytes 62208 | tf_op jit(solution)/shard_map/psum | solution.py:404
  1116.3 71.9 %all-reduce.20.cloned.1.call-done = (f32[768,192]{0,1:T(8,128)}, f32[768,192]{0,1:T(8,128)}, f32[768,192]{0,1:T(8,128)}, f32[768,192]{0,1:T(8,128)}) async-done(((f32[768,192]{0,1:T(8,128)}, f32[768,192]{0,1:T(8,128)}, f32[768,192]{0,1:T(8,128)}, f32[768,192]{0,1:T(8,128)}), (f32[768,192]{0,1:T(8,128)}, f32[768,192]{0,1:T(8,128)}, f32[768,192]{0,1:T(8,128)}, ...) | async-done | bytes 2359312 | tf_op jit(solution)/shard_map/psum | solution.py:404
  (269 shorter events, 101.6 us)
Async XLA Ops:
  7.2 432.6 %copy-start = (bf16[1,768,768]{2,1,0:T(8,128)(2,1)S(1)}, bf16[1,768,768]{2,1,0:T(8,128)(2,1)}, u32[]{:S(2)}) copy-start(bf16[1,768,768]{2,1,0:T(8,128)(2,1)} %param.34) | copy-start | bytes 3538948
  7.2 68.2 %copy-start.16 = (bf16[1,512,768]{2,1,0:T(8,128)(2,1)S(1)}, bf16[1,512,768]{2,1,0:T(8,128)(2,1)}, u32[]{:S(2)}) copy-start(bf16[1,512,768]{2,1,0:T(8,128)(2,1)} %param.23) | copy-start | bytes 2359300
  7.2 68.2 %copy-start.60 = (f32[768]{0:T(1024)S(1)}, f32[768]{0:T(1024)}, u32[]{:S(2)}) copy-start(f32[768]{0:T(1024)} %param.24) | copy-start | bytes 9220
  7.2 363.9 %all-reduce.14.cloned.1.call-start = ((), (), s32[]{:S(2)}) async-start(), calls=%async_computation.6 | async-start | bytes 3145728 | tf_op jit(solution)/shard_map/psum | solution.py:182
  9.4 186.7 %copy-start.57 = (f32[512]{0:T(512)}, f32[512]{0:T(512)S(1)}, u32[]{:S(2)}) copy-start(f32[512]{0:T(512)S(1)} %get-tuple-element.1269) | copy-start | bytes 6148
  42.3 33.6 %copy-start.44 = (bf16[768,192]{1,0:T(8,128)(2,1)}, bf16[768,192]{1,0:T(8,128)(2,1)S(1)}, u32[]{:S(2)}) copy-start(bf16[768,192]{1,0:T(8,128)(2,1)S(1)} %all_gather.22) | copy-start | bytes 884740
  73.6 8.8 copy-start.42
  73.6 8.8 copy-start.47
  73.6 8.8 copy-start.66
  82.4 41.5 %copy-start.53 = (bf16[96,192]{1,0:T(8,128)(2,1)S(1)}, bf16[96,192]{1,0:T(8,128)(2,1)}, u32[]{:S(2)}) copy-start(bf16[96,192]{1,0:T(8,128)(2,1)} %param.27) | copy-start | bytes 110596
  116.7 3.6 copy-start.2
  116.7 3.6 copy-start.5
  123.9 81.5 %copy-start.54 = (bf16[96,192]{1,0:T(8,128)(2,1)S(1)}, bf16[96,192]{1,0:T(8,128)(2,1)}, u32[]{:S(2)}) copy-start(bf16[96,192]{1,0:T(8,128)(2,1)} %param.28) | copy-start | bytes 110596
  273.3 3.7 copy-start.3
  273.3 3.7 copy-start.12
  273.3 3.7 copy-start.22
  273.4 3.7 copy-start.40
  282.3 2.9 copy-start.32
  282.3 2.7 copy-start.52
  282.3 2.7 copy-start.59
  282.3 88.8 %copy-start.17 = (bf16[1,512,768]{2,1,0:T(8,128)(2,1)S(1)}, bf16[1,512,768]{2,1,0:T(8,128)(2,1)}, u32[]{:S(2)}) copy-start(bf16[1,512,768]{2,1,0:T(8,128)(2,1)} %param.23) | copy-start | bytes 2359300
  285.4 88.6 %copy-start.56 = (f32[768]{0:T(1024)S(1)}, f32[768]{0:T(1024)}, u32[]{:S(2)}) copy-start(f32[768]{0:T(1024)} %param.31) | copy-start | bytes 9220
  383.8 52.4 %copy-start.64 = (bf16[1,768,768]{2,1,0:T(8,128)(2,1)S(1)}, bf16[1,768,768]{2,1,0:T(8,128)(2,1)}, u32[]{:S(2)}) copy-start(bf16[1,768,768]{2,1,0:T(8,128)(2,1)} %param.33) | copy-start | bytes 3538948
  437.9 1.9 copy-start.67
  516.0 50.4 %all-to-all-start.1 = ((bf16[8,160,768]{2,1,0:T(8,128)(2,1)}), bf16[8,160,768]{2,1,0:T(8,128)(2,1)S(1)}, u32[]{:S(2)}, u32[]{:S(2)}) async-start(bf16[8,160,768]{2,1,0:T(8,128)(2,1)} %all-reduce.21), calls=%async_computation.1 | async-start | bytes 3932160 | tf_op jit(solution)/shard_map/all_to_all | solution.py:210
  524.8 5.3 copy-start.55
  582.9 49.7 %copy-start.68 = (f32[8,160,768]{2,1,0:T(8,128)S(1)}, f32[8,160,768]{2,1,0:T(8,128)}, u32[]{:S(2)}) copy-start(f32[8,160,768]{2,1,0:T(8,128)} %copy-done.67) | copy-start | bytes 11796484
  632.6 3.7 copy-start.29
  632.6 5.0 copy-start.65
  640.6 4.5 copy-start.15
  640.6 48.8 %all-to-all-start.3 = ((bf16[8,160,768]{2,1,0:T(8,128)(2,1)}), bf16[8,160,768]{2,1,0:T(8,128)(2,1)}, u32[]{:S(2)}, u32[]{:S(2)}) async-start(bf16[8,160,768]{2,1,0:T(8,128)(2,1)} %convolution_convert_fusion), calls=%async_computation.3 | async-start | bytes 3932160 | tf_op jit(solution)/shard_map/all_to_all | solution.py:248
  645.1 107.0 %all-reduce.16.cloned.1.call-start = ((), (), s32[]{:S(2)}) async-start(), calls=%async_computation.7 | async-start | bytes 1572864 | tf_op jit(solution)/shard_map/psum | solution.py:266
  701.0 5.2 copy-start.28
  706.2 45.8 %copy-start.9 = (f32[512,768]{1,0:T(8,128)S(1)}, f32[512,768]{1,0:T(8,128)}, u32[]{:S(2)}) copy-start(f32[512,768]{1,0:T(8,128)} %copy-done.8) | copy-start | bytes 4718596
  719.1 299.8 %reduce-scatter.3.cloned.1.call-start = ((), (), s32[]{:S(2)}) async-start(), calls=%async_computation.8 | async-start | bytes 589824 | tf_op jit(solution)/shard_map/reduce_scatter | solution.py:366
  719.2 35.4 %copy-start.50 = (bf16[512,8]{0,1:T(8,128)(2,1)}, bf16[512,8]{0,1:T(8,128)(2,1)S(1)}, u32[]{:S(2)}) copy-start(bf16[512,8]{0,1:T(8,128)(2,1)S(1)} %select_reduce_fusion.1) | copy-start | bytes 24580
  719.2 35.4 %copy-start.25 = (bf16[1,512,768]{2,1,0:T(8,128)(2,1)S(1)}, bf16[1,512,768]{2,1,0:T(8,128)(2,1)}, u32[]{:S(2)}) copy-start(bf16[1,512,768]{2,1,0:T(8,128)(2,1)} %param.37) | copy-start | bytes 2359300
  752.0 2.6 copy-start.23
  754.6 2.5 copy-start.24
  756.0 1.6 copy-start.4
  793.6 3.6 copy-start.13
  859.1 3.0 copy-start.36
  864.2 1.4 copy-start.10
  865.9 5.8 copy-start.11
  892.2 4.0 copy-start.18
  892.2 4.0 copy-start.58
  892.2 4.0 copy-start.61
  892.2 142.7 %reduce-scatter.5.cloned.1.call-start = ((), (), s32[]{:S(2)}) async-start(), calls=%async_computation.9 | async-start | bytes 589824 | tf_op jit(solution)/shard_map/reduce_scatter | solution.py:372
  893.4 4.1 copy-start.7
  893.4 4.1 copy-start.33
  896.1 122.9 %copy-start.43 = (bf16[768,192]{1,0:T(8,128)(2,1)S(1)}, bf16[768,192]{1,0:T(8,128)(2,1)}, u32[]{:S(2)}) copy-start(bf16[768,192]{1,0:T(8,128)(2,1)} %copy-done.42) | copy-start | bytes 884740
  896.1 176.9 %all-reduce.18.cloned.1.call-start = ((), (), s32[]{:S(2)}) async-start(), calls=%async_computation.10 | async-start | bytes 1572864 | tf_op jit(solution)/shard_map/psum | solution.py:394
  897.5 137.4 %copy-start.35 = (bf16[768,192]{1,0:T(8,128)(2,1)S(1)}, bf16[768,192]{1,0:T(8,128)(2,1)}, u32[]{:S(2)}) copy-start(bf16[768,192]{1,0:T(8,128)(2,1)} %copy-done.34) | copy-start | bytes 884740
  1021.4 16.8 %copy-start.49 = (bf16[1,512,192]{1,2,0:T(8,128)(2,1)S(1)}, bf16[1,512,192]{1,2,0:T(8,128)(2,1)}, u32[]{:S(2)}) copy-start(bf16[1,512,192]{1,2,0:T(8,128)(2,1)} %reduce-scatter.3.cloned.1.call-done) | copy-start | bytes 589828
  1038.1 1.4 copy-start.48
  1038.2 150.1 %all-reduce.20.cloned.1.call-start = ((), (), s32[]{:S(2)}) async-start(), calls=%async_computation.11 | async-start | bytes 4718592 | tf_op jit(solution)/shard_map/psum | solution.py:404
  1041.0 5.5 copy-start.30
  1041.0 5.5 copy-start.69
  1046.5 28.4 %copy-start.62 = (f32[768]{0:T(1024)S(1)}, f32[768]{0:T(1024)}, u32[]{:S(2)}) copy-start(f32[768]{0:T(1024)} %get-tuple-element.1144) | copy-start | bytes 9220
  1046.5 68.2 %copy-start.63 = (f32[512]{0:T(512)S(1)}, f32[512]{0:T(512)}, u32[]{:S(2)}) copy-start(f32[512]{0:T(512)} %get-tuple-element.1268) | copy-start | bytes 6148
  1073.0 41.8 %copy-start.26 = (bf16[512,768]{1,0:T(8,128)(2,1)S(1)}, bf16[512,768]{1,0:T(8,128)(2,1)}, u32[]{:S(2)}) copy-start(bf16[512,768]{1,0:T(8,128)(2,1)} %all-reduce.18.cloned.1.call-done) | copy-start | bytes 2359300
  1188.2 4.0 copy-start.46
  1188.2 4.8 copy-start.45
  1188.2 5.6 copy-start.1
  (14 other events, 14.2 us)
Sparse Core Ops, SparseCore 0:
  285.1 85.9 all-reduce.13
  719.2 32.7 all-reduce.15
  892.3 126.5 reduce-scatter.2
  1021.7 13.1 reduce-scatter.4
  1038.3 34.6 all-reduce.17
  1077.3 110.8 all-reduce.19
where the time goes:
time: 1220 us; the launch traced here: 1200 us
  waiting for transfers between devices  425 us (35%)
  blocking collectives  395 us (32%)
  local copies, waits for them, and re-layouts  222 us (18%)
  matrix products  66.7 us (5%)
  other arithmetic  49.2 us (4%)
  loops' own time  19.6 us (2%)
  between operations  15.2 us (1%)
    reduce_scatter x1, waiting for transfers between devices, on_device(): lax.psum_scatter(keys_part.reshape(sequences, length, heads_local * head_...  120 us
    psum x1, waiting for transfers between devices, on_device(): hidden_one = source + lax.psum(branch, 'tensor')  85.8 us
    all_gather x1, blocking collectives, on_device(): lax.all_gather(w_value, ('dp', 'ctx'), axis=0, tiled=True)  72.1 us
    psum x1, waiting for transfers between devices, on_device(): lax.psum((grad_gain_one, grad_gain_two, grad_router, grad_table, weight_g...  71.9 us
    psum x1, blocking collectives, on_device(): produced = lax.psum(partial_out, 'tensor').astype(jnp.bfloat16)  71.9 us
    while x45, local copies, waits for them, and re-layouts  67.7 us
    reshape x4, local copies, waits for them, and re-layouts, toeplitz(): skewed = tiled[:, :height * span].reshape(heads, height, span)  53 us
    all_to_all x1, blocking collectives, on_device(): lax.all_to_all(outgoing, ('dp', 'ctx'), split_axis=0, concat_axis=0, tile...  51.1 us
  transfers between devices with their start and end apart: 8, of which 8 were waited for; matrix products, arithmetic and copies ran while one was open for 3% of the time, Pallas kernels for 0%

commit v1 on v0

v1 whole, which is shorter than its diff:
```python
import functools

import jax
import jax.numpy as jnp
from jax import lax
from jax.experimental import pallas as pl
from jax.experimental.pallas import tpu as pltpu
from jax.sharding import PartitionSpec as P

EPS = 1e-06
MASKED = -1e30
SUB = 128
F32 = jnp.float32
BF16 = jnp.bfloat16


def dot(a, b, ca=1, cb=0):
    return lax.dot_general(a, b, (((ca,), (cb,)), ((), ())), preferred_element_type=F32)


def lane_distance(delta, rows, v):
    span = 2 * rows
    v = jnp.where(v > span - SUB, v - span, v)
    return delta * rows + rows - SUB - v


def bias_band(delta, rows, heads, starts_ref, table_ref, band_ref):
    span = 2 * rows
    far = lane_distance(delta, rows, lax.broadcasted_iota(jnp.int32, (8, span), 1))
    lines = [jnp.full((8, span), MASKED, F32) for _ in range(heads)]
    for b in range(table_ref.shape[0]):
        reached = far >= starts_ref[b]
        for h in range(heads):
            lines[h] = jnp.where(reached, table_ref[b, h], lines[h])
    for h in range(heads):
        wide = jnp.broadcast_to(lines[h][0:1], (SUB, span))
        band_ref[h] = pltpu.roll(wide, 0, 1, stride=1, stride_axis=0)


def forward_kernel(
    heads, ctx_ref, starts_ref, table_ref, q_ref, k_ref, v_ref,
    mixed_ref, wide_ref, log_ref, band_ref, peak_ref, total_ref,
):
    rows = q_ref.shape[0]
    dim = q_ref.shape[1] // heads
    me = ctx_ref[0]
    peak_ref[...] = jnp.full_like(peak_ref, MASKED)
    total_ref[...] = jnp.zeros_like(total_ref)
    wide_ref[...] = jnp.zeros_like(wide_ref)

    def step_fn(step, carry):
        bias_band(me - step, rows, heads, starts_ref, table_ref, band_ref)
        at = pl.multiple_of(step * rows, rows)
        for h in range(heads):
            cols = slice(h * dim, (h + 1) * dim)
            keys = k_ref[pl.ds(at, rows), cols]
            values = v_ref[pl.ds(at, rows), cols]
            for a in range(rows // SUB):
                mine = slice(a * SUB, (a + 1) * SUB)
                off = rows - SUB - SUB * a
                query = q_ref[mine, cols] * BF16(dim ** -0.5)
                logits = dot(query, keys, 1, 1) + band_ref[h, :, off : off + rows]
                old = peak_ref[h, mine, :]
                new = jnp.maximum(old, jnp.max(logits, axis=1, keepdims=True))
                shares = jnp.exp(logits - new)
                shrink = jnp.exp(old - new)
                peak_ref[h, mine, :] = new
                total_ref[h, mine, :] = total_ref[h, mine, :] * shrink + jnp.sum(
                    shares, axis=1, keepdims=True
                )
                wide_ref[mine, cols] = wide_ref[mine, cols] * shrink + dot(
                    shares.astype(BF16), values
                )
        return carry

    lax.fori_loop(0, me + 1, step_fn, 0)
    for h in range(heads):
        cols = slice(h * dim, (h + 1) * dim)
        total = total_ref[h]
        mixed = wide_ref[:, cols] / total
        wide_ref[:, cols] = mixed
        mixed_ref[:, cols] = mixed.astype(BF16)
        log_ref[:, h : h + 1] = peak_ref[h] + jnp.log(total)


def backward_kernel(
    heads, ctx_ref, starts_ref, table_ref, q_ref, k_ref, v_ref, g_ref, wide_ref, log_ref,
    dq_ref, dk_ref, dv_ref, diag_ref, band_ref, sums_ref, dlogit_ref, share_ref, acc_ref,
):
    rows = q_ref.shape[0]
    span = 2 * rows
    dim = q_ref.shape[1] // heads
    me = ctx_ref[0]
    dk_ref[...] = jnp.zeros_like(dk_ref)
    dv_ref[...] = jnp.zeros_like(dv_ref)
    diag_ref[...] = jnp.zeros_like(diag_ref)
    acc_ref[...] = jnp.zeros_like(acc_ref)

    def step_fn(step, carry):
        delta = me - step
        bias_band(delta, rows, heads, starts_ref, table_ref, band_ref)
        at = pl.multiple_of(step * rows, rows)
        for h in range(heads):
            cols = slice(h * dim, (h + 1) * dim)
            keys = k_ref[pl.ds(at, rows), cols]
            values = v_ref[pl.ds(at, rows), cols]
            sums_ref[...] = jnp.zeros_like(sums_ref)
            for a in range(rows // SUB):
                mine = slice(a * SUB, (a + 1) * SUB)
                off = rows - SUB - SUB * a
                query = q_ref[mine, cols] * BF16(dim ** -0.5)
                grad = g_ref[mine, cols]
                inner = jnp.sum(grad.astype(F32) * wide_ref[mine, cols], axis=1, keepdims=True)
                logits = dot(query, keys, 1, 1) + band_ref[h, :, off : off + rows]
                shares = jnp.exp(logits - log_ref[mine, h : h + 1])
                dlogits = shares * (dot(grad, values, 1, 1) - inner)
                sums_ref[:, off : off + rows] += dlogits
                low = dlogits.astype(BF16)
                share_ref[mine, :] = shares.astype(BF16)
                dlogit_ref[mine, :] = low
                acc_ref[mine, cols] += dot(low, keys)
            dk_ref[pl.ds(at, rows), cols] = (
                dot(dlogit_ref[...], q_ref[:, cols], 0, 0) * dim ** -0.5
            ).astype(BF16)
            dv_ref[pl.ds(at, rows), cols] = dot(share_ref[...], g_ref[:, cols], 0, 0).astype(BF16)
            folded = sums_ref[...]
            width = SUB // 2
            while width >= 8:
                folded = folded[:width] + pltpu.roll(folded[width:], span - width, 1)
                width //= 2
            diag_ref[h, delta] = folded
        return carry

    lax.fori_loop(0, me + 1, step_fn, 0)
    dq_ref[...] = (acc_ref[...] * dim ** -0.5).astype(BF16)


def specs(*kinds):
    return [pl.BlockSpec(memory_space=pltpu.SMEM if k == "s" else pltpu.VMEM) for k in kinds]


def attend_forward(me, starts, table, query, keys, values):
    rows, width = query.shape
    heads = table.shape[1]
    return pl.pallas_call(
        functools.partial(forward_kernel, heads),
        out_shape=(
            jax.ShapeDtypeStruct((rows, width), BF16),
            jax.ShapeDtypeStruct((rows, width), F32),
            jax.ShapeDtypeStruct((rows, heads), F32),
        ),
        in_specs=specs(*"sssvvv"),
        out_specs=tuple(specs(*"vvv")),
        scratch_shapes=[
            pltpu.VMEM((heads, SUB, 2 * rows), F32),
            pltpu.VMEM((heads, rows, 1), F32),
            pltpu.VMEM((heads, rows, 1), F32),
        ],
        compiler_params=pltpu.CompilerParams(vmem_limit_bytes=40 * 2**20),
        name="attend_forward",
    )(me, starts, table, query, keys, values)


def attend_backward(me, starts, table, query, keys, values, grad, wide, logs):
    rows, width = query.shape
    length = keys.shape[0]
    heads = table.shape[1]
    return pl.pallas_call(
        functools.partial(backward_kernel, heads),
        out_shape=(
            jax.ShapeDtypeStruct((rows, width), BF16),
            jax.ShapeDtypeStruct((length, width), BF16),
            jax.ShapeDtypeStruct((length, width), BF16),
            jax.ShapeDtypeStruct((heads, length // rows, 8, 2 * rows), F32),
        ),
        in_specs=specs(*"sssvvvvvv"),
        out_specs=tuple(specs(*"vvvv")),
        scratch_shapes=[
            pltpu.VMEM((heads, SUB, 2 * rows), F32),
            pltpu.VMEM((SUB, 2 * rows), F32),
            pltpu.VMEM((rows, rows), BF16),
            pltpu.VMEM((rows, rows), BF16),
            pltpu.VMEM((rows, width), F32),
        ],
        compiler_params=pltpu.CompilerParams(vmem_limit_bytes=40 * 2**20),
        name="attend_backward",
    )(me, starts, table, query, keys, values, grad, wide, logs)


def table_grad(diag, starts):
    heads, blocks, sub, span = diag.shape
    delta = lax.broadcasted_iota(jnp.int32, (blocks, sub, span), 0)
    row = lax.broadcasted_iota(jnp.int32, (blocks, sub, span), 1)
    lane = lax.broadcasted_iota(jnp.int32, (blocks, sub, span), 2)
    far = lane_distance(delta, span // 2, lane) + row
    later = jnp.concatenate([starts[1:], jnp.full((1,), 2**30, jnp.int32)])
    inside = (far[None] >= starts[:, None, None, None]) & (far[None] < later[:, None, None, None])
    return jnp.sum(
        jnp.where(inside[:, None], diag[None], 0.0), axis=(2, 3, 4)
    )


def hi_lo(x):
    hi = x.astype(BF16)
    return hi, (x - hi.astype(F32)).astype(BF16)


def norm_scale(value):
    return lax.rsqrt(jnp.mean(value * value, axis=-1, keepdims=True) + EPS)


def norm_backward(value, scale, gain, grad_normed):
    scaled = grad_normed * gain
    grad_value = scale * scaled - value * scale**3 * jnp.mean(
        value * scaled, axis=-1, keepdims=True
    )
    return grad_value, jnp.sum(grad_normed * value * scale, axis=0)


def sum_groups(grad):
    part = lax.psum_scatter(grad.astype(BF16), ("dp", "ctx"), scatter_dimension=0, tiled=True)
    return lax.all_gather(part, ("dp", "ctx"), axis=0, tiled=True).astype(F32)


def on_device(
    inputs, gain_attention, w_query, w_key, w_value, w_output, bias_table, bucket_start,
    gain_experts, w_router, w_up, w_down, expert_ids, slot_index, cotangent,
):
    sequences, rows, width = inputs.shape
    tokens = sequences * rows
    experts = w_router.shape[1]
    top = expert_ids.shape[2]
    capacity = 5 * tokens * top // (4 * experts)
    heads = bias_table.shape[1]
    split = lax.axis_size("tensor")
    ctxs = lax.axis_size("ctx")
    at_tensor = lax.axis_index("tensor")
    at_ctx = lax.axis_index("ctx")
    me = at_ctx.astype(jnp.int32).reshape(1)
    part = tokens // split
    slots = capacity // split
    shard_rows = experts * slots
    groups = ("dp", "ctx")

    def my_tokens(x):
        return lax.dynamic_slice_in_dim(x, at_tensor * part, part, 0)

    def gather_tensor(x):
        return lax.all_gather(x, "tensor", axis=0, tiled=True)

    def scatter_tensor(x):
        return lax.psum_scatter(x.astype(BF16), "tensor", scatter_dimension=0, tiled=True)

    def exchange(x):
        return lax.all_to_all(x, groups, split_axis=0, concat_axis=0, tiled=True)

    route = expert_ids.reshape(tokens, top)
    place = slot_index.reshape(tokens, top)
    local = place - at_tensor * slots
    inside = (place >= 0) & (local >= 0) & (local < slots)
    row_of = jnp.where(inside, route * slots + local, -1)
    spots = jnp.arange(shard_rows, dtype=jnp.int32)
    hits = [row_of[:, k : k + 1] == spots[None, :] for k in range(top)]
    ones = [h.astype(BF16) for h in hits]
    any_hit = sum(ones[1:], ones[0])
    cot = cotangent.reshape(tokens, width)

    qkv_w = lax.all_gather(
        jnp.concatenate([w_query, w_key, w_value], axis=1), groups, axis=0, tiled=True
    )
    output_w = lax.all_gather(w_output, groups, axis=0, tiled=True)
    cot_rows = gather_tensor(exchange(dot(any_hit, cot, 0, 0).astype(BF16)))
    source = inputs.astype(F32).reshape(tokens, width)
    scale_one = norm_scale(source)
    normed_one = (source * scale_one * gain_attention).astype(BF16)
    hh = w_query.shape[1]
    qkv = dot(normed_one, qkv_w).astype(BF16).reshape(sequences, rows, 3 * hh)
    kv_all = lax.all_gather(qkv[:, :, hh:], "ctx", axis=1, tiled=True)
    seen = [
        attend_forward(
            me, bucket_start, bias_table,
            qkv[b, :, :hh], kv_all[b, :, :hh], kv_all[b, :, hh:],
        )
        for b in range(sequences)
    ]
    mixed = jnp.concatenate([s[0] for s in seen], axis=0)
    source_mine = my_tokens(source)
    hidden = source_mine + scatter_tensor(dot(mixed, output_w, 1, 1)).astype(F32)
    scale_two = norm_scale(hidden)
    normed_mine = (hidden * scale_two * gain_experts).astype(BF16)
    normed_two = gather_tensor(normed_mine)

    router_logits = dot(normed_two, w_router)
    picks = route[:, :, None] == jnp.arange(experts, dtype=jnp.int32)[None, None, :]
    chosen = jnp.sum(jnp.where(picks, router_logits[:, None, :], 0.0), axis=-1)
    gates = jax.nn.softmax(chosen, axis=-1)
    row_gate = sum(
        jnp.sum(jnp.where(hits[k], gates[:, k : k + 1], 0.0), axis=0) for k in range(top)
    )

    gate_hi, gate_lo = hi_lo(row_gate[:, None])
    sent = jnp.concatenate(
        [
            dot(any_hit, normed_two, 0, 0).astype(BF16),
            jnp.broadcast_to(gate_hi, (shard_rows, 64)),
            jnp.broadcast_to(gate_lo, (shard_rows, 64)),
        ],
        axis=1,
    )
    arrived = gather_tensor(exchange(sent))
    buffer = arrived[:, :width]
    gate_rows = arrived[:, width : width + 1].astype(F32) + arrived[
        :, width + 64 : width + 65
    ].astype(F32)
    grad_produced = (gate_rows * cot_rows.astype(F32)).astype(BF16)
    up, down = w_up[0], w_down[0]
    before = dot(buffer, up)
    activated, gelu_pullback = jax.vjp(jax.nn.gelu, before)
    activated = activated.astype(BF16)
    returned = exchange(scatter_tensor(dot(activated, down)))
    grad_before = gelu_pullback(dot(grad_produced, down, 1, 1))[0].astype(BF16)
    grad_returned = exchange(scatter_tensor(dot(grad_before, up, 1, 1)))
    grad_down = dot(activated, grad_produced, 0, 0)
    grad_up = dot(buffer, grad_before, 0, 0)

    cot32 = cot.astype(F32)
    picked = [dot(one, returned) for one in ones]
    mixture = sum(gates[:, k : k + 1] * picked[k] for k in range(top))
    gate_part = jnp.stack([jnp.sum(cot32 * picked[k], axis=-1) for k in range(top)], axis=1)
    part_hi, part_lo = hi_lo(gate_part)
    summed = scatter_tensor(
        jnp.concatenate(
            [
                mixture.astype(BF16),
                dot(any_hit, grad_returned).astype(BF16),
                jnp.pad(jnp.concatenate([part_hi, part_lo], axis=1), ((0, 0), (0, 128 - 2 * top))),
            ],
            axis=1,
        )
    ).astype(F32)
    result = hidden + summed[:, :width]
    layer_out = gather_tensor(result.astype(BF16))
    grad_gates = (
        summed[:, 2 * width : 2 * width + top] + summed[:, 2 * width + top : 2 * width + 2 * top]
    )
    gates_mine = my_tokens(gates)
    grad_chosen = gates_mine * (
        grad_gates - jnp.sum(gates_mine * grad_gates, axis=-1, keepdims=True)
    )
    grad_logits = jnp.sum(
        jnp.where(my_tokens(picks), grad_chosen[:, :, None], 0.0), axis=1
    ).astype(BF16)
    grad_router = dot(normed_mine, grad_logits, 0, 0)
    grad_normed_two = summed[:, width : 2 * width] + dot(grad_logits, w_router, 1, 1)
    grad_back, grad_gain_two = norm_backward(hidden, scale_two, gain_experts, grad_normed_two)
    grad_hidden = my_tokens(cot).astype(F32) + grad_back
    grad_branch = gather_tensor(grad_hidden.astype(BF16))

    grad_mixed = dot(grad_branch, output_w).astype(BF16).reshape(sequences, rows, hh)
    grad_output = sum_groups(dot(grad_branch, mixed, 0, 0))
    back = [
        attend_backward(
            me, bucket_start, bias_table,
            qkv[b, :, :hh], kv_all[b, :, :hh], kv_all[b, :, hh:],
            grad_mixed[b], seen[b][1], seen[b][2],
        )
        for b in range(sequences)
    ]
    kv_part = jnp.stack([jnp.concatenate([b[1], b[2]], axis=1) for b in back])
    kv_grad = lax.psum_scatter(kv_part, "ctx", scatter_dimension=1, tiled=True)
    qkv_grad = jnp.concatenate([jnp.stack([b[0] for b in back]), kv_grad], axis=2).reshape(
        tokens, 3 * hh
    )
    grad_table = sum(table_grad(b[3], bucket_start) for b in back)
    grad_normed_one = scatter_tensor(dot(qkv_grad, qkv_w, 1, 1)).astype(F32)
    grad_qkv_w = sum_groups(dot(normed_one, qkv_grad, 0, 0))
    grad_back_one, grad_gain_one = norm_backward(
        source_mine, my_tokens(scale_one), gain_attention, grad_normed_one
    )
    grad_inputs = gather_tensor((grad_hidden + grad_back_one).astype(BF16)).astype(F32)

    small = lax.psum(
        jnp.concatenate([grad_gain_one[:, None], grad_gain_two[:, None], grad_router], axis=1).T,
        ("dp", "ctx", "tensor"),
    )
    grad_table = lax.psum(grad_table, groups)
    return (
        layer_out.reshape(sequences, rows, width),
        grad_inputs.reshape(sequences, rows, width),
        small[0],
        grad_qkv_w[:, :hh],
        grad_qkv_w[:, hh : 2 * hh],
        grad_qkv_w[:, 2 * hh :],
        grad_output,
        grad_table,
        small[1],
        small[2:].T,
        grad_up[None],
        grad_down[None],
    )


def solution(mesh):
    in_specs = (
        P("dp", "ctx", None),
        P(),
        P(("dp", "ctx"), "tensor"),
        P(("dp", "ctx"), "tensor"),
        P(("dp", "ctx"), "tensor"),
        P(("dp", "ctx"), "tensor"),
        P(None, "tensor"),
        P(),
        P(),
        P(),
        P(("dp", "ctx"), None, "tensor"),
        P(("dp", "ctx"), "tensor", None),
        P("dp", "ctx", None),
        P("dp", "ctx", None),
        P("dp", "ctx", None),
    )
    out_specs = (
        P("dp", "ctx", None),
        P("dp", "ctx", None),
        P(),
        P(None, "tensor"),
        P(None, "tensor"),
        P(None, "tensor"),
        P(None, "tensor"),
        P(None, "tensor"),
        P(),
        P(),
        P(("dp", "ctx"), None, "tensor"),
        P(("dp", "ctx"), "tensor", None),
    )
    return jax.shard_map(
        on_device, mesh=mesh, in_specs=in_specs, out_specs=out_specs, check_vma=False
    )
```

time: 1220 us -> 596 us (0.49)
  waiting for transfers between devices: 425 us -> 158 us
  local copies, waits for them, and re-layouts: 222 us -> 36.1 us
  blocking collectives: 395 us -> 285 us
  other arithmetic: 49.2 us -> 18.7 us
  loops' own time: 19.6 us -> 0 us
  matrix products: 66.7 us -> 51.5 us
  Pallas kernels: 0 us -> 13.1 us
    psum x4 -> x0, waiting for transfers between devices: 213 us -> none  [the longest x1 85.8 us: on_device(): hidden_one = source + lax.psum(branch, 'tensor')]
    all_to_all x2, waiting for transfers between devices: 77.5 us -> 9.24 us  [exchange(): return lax.all_to_all(x, groups, split_axis=0, concat_axis=0, tiled=True)]
    while x45 -> x0, local copies, waits for them, and re-layouts: 67.7 us -> none
    all_to_all x2, blocking collectives: 101 us -> 38.8 us  [exchange(): return lax.all_to_all(x, groups, split_axis=0, concat_axis=0, tiled=True)]
    reshape x6 -> x0, local copies, waits for them, and re-layouts: 60 us -> none  [the longest x4 53 us: toeplitz(): skewed = tiled[:, :height * span].reshape(heads, height, span)]
    reduce_scatter x2 -> x5, waiting for transfers between devices: 134 us -> 86.5 us  [the longest x2 50.9 us: scatter_tensor(): lax.psum_scatter(x.astype(BF16), 'tensor', scatter_dimension=0, tiled=True)]
    unnamed x6 -> x13, waiting for transfers between devices: 0.1 us -> 45.9 us
    psum x2, blocking collectives: 112 us -> 73.5 us  [the longest x1 37.3 us: on_device(): lax.psum(jnp.concatenate([grad_gain_one[:, None], grad_gain_two[:, None],...]
  transfers between devices with their start and end apart: 8 -> 12, of which waited for: 8 -> 10; matrix products, arithmetic and copies ran while one was open for 3% -> 11% of each run, Pallas kernels for 0% -> 0%
where the time goes in v1:
time: 596 us; the launch traced here: 589 us
  blocking collectives  285 us (48%)
  waiting for transfers between devices  158 us (27%)
  matrix products  51.5 us (9%)
  local copies, waits for them, and re-layouts  36.1 us (6%)
  other arithmetic  18.7 us (3%)
  between operations  15.3 us (3%)
  Pallas kernels  13.1 us (2%)
  starting transfers between devices  11.9 us (2%)
    all_gather x2, blocking collectives, sum_groups(): return lax.all_gather(part, ('dp', 'ctx'), axis=0, tiled=True).astype(F32)  64.3 us
    dot_general x20, matrix products, dot(): lax.dot_general(a, b, (((ca,), (cb,)), ((), ())), preferred_element_type=...  51.5 us
    reduce_scatter x2, waiting for transfers between devices, scatter_tensor(): lax.psum_scatter(x.astype(BF16), 'tensor', scatter_dimension=0, tiled=True)  50.9 us
    unnamed x13, waiting for transfers between devices  45.9 us
    all_to_all x2, blocking collectives, exchange(): return lax.all_to_all(x, groups, split_axis=0, concat_axis=0, tiled=True)  38.8 us
    psum x1, blocking collectives, on_device(): lax.psum(jnp.concatenate([grad_gain_one[:, None], grad_gain_two[:, None],...  37.3 us
    psum x1, blocking collectives, on_device(): grad_table = lax.psum(grad_table, groups)  36.2 us
    all_gather x1, blocking collectives, on_device(): lax.all_gather(jnp.concatenate([w_query, w_key, w_value], axis=1), groups...  34.4 us
  transfers between devices with their start and end apart: 12, of which 10 were waited for; matrix products, arithmetic and copies ran while one was open for 11% of the time, Pallas kernels for 0%

profile of v1, /device:TPU:0, one launch (start us, length us, event | category | flops | bytes accessed | tf_op | source)
XLA Modules:
  0.0 588.6 jit_solution(1258850974860956097)
XLA Ops:
  7.3 1.5 fusion.18
  9.7 34.4 %all_gather.33 = bf16[768,576]{1,0:T(8,128)(2,1)S(1)} all-gather(bf16[96,576]{1,0:T(8,128)(2,1)S(1)} %pad_maximum_fusion.1), channel_id=1, replica_groups=mesh['dp'=4,'ctx'=2,'tensor'=4] {'dp','ctx'}, dimensions={0}, use_global_device_ids=true | all-gather | bytes 995328 | tf_op jit(solution)/shard_map/all_gather | solution.py:268
  45.4 31.2 %all_gather.35 = bf16[768,192]{1,0:T(8,128)(2,1)S(1)} all-gather(bf16[96,192]{1,0:T(8,128)(2,1)S(1)} %copy-done.33), channel_id=1, replica_groups=mesh['dp'=4,'ctx'=2,'tensor'=4] {'dp','ctx'}, dimensions={0}, use_global_device_ids=true | all-gather | bytes 331776 | tf_op jit(solution)/shard_map/all_gather | solution.py:271
  76.6 8.4 %all_gather.34 = bf16[1,1024,384]{2,1,0:T(8,128)(2,1)S(1)} all-gather(bf16[1,512,384]{2,1,0:T(8,128)(2,1)S(1)} %slice.94), channel_id=1, replica_groups=mesh['dp'=4,'ctx'=2,'tensor'=4] {'ctx'}, dimensions={1}, use_global_device_ids=true | all-gather | bytes 1179648 | tf_op jit(solution)/shard_map/all_gather | solution.py:278
  85.9 5.8 attend_forward.1
  91.7 1.3 convolution_convert_fusion.5
  93.1 2.4 convert_element_type.149
  95.5 1.8 constant_dynamic-slice_fusion.2
  97.3 1.9 copy.106
  100.0 21.9 %reduce-scatter.25.cloned.1.call-done = bf16[128,768]{1,0:T(8,128)(2,1)} async-done(((bf16[512,768]{1,0:T(8,128)(2,1)}), bf16[128,768]{1,0:T(8,128)(2,1)}) %reduce-scatter.25.cloned.1.call-update) | async-done | bytes 196624
  122.9 1.2 multiply_reduce_fusion.2
  124.1 1.2 multiply_convert_fusion.5
  125.3 8.2 %all_gather.36 = bf16[512,768]{0,1:T(8,128)(2,1)S(1)} all-gather(bf16[128,768]{0,1:T(8,128)(2,1)S(1)} %multiply_convert_fusion.5), channel_id=1, replica_groups=mesh['dp'=4,'ctx'=2,'tensor'=4] {'tensor'}, dimensions={0}, use_global_device_ids=true | all-gather | bytes 983040 | tf_op jit(solution)/shard_map/all_gather | solution.py:249
  134.8 1.6 convolution_convert_fusion.8
  136.9 22.2 %all_to_all.48 = bf16[8,40,896]{2,1,0:T(8,128)(2,1)} all-to-all(bf16[8,40,896]{2,1,0:T(8,128)(2,1)S(1)} %bitcast.146), channel_id=1, replica_groups=mesh['dp'=4,'ctx'=2,'tensor'=4] {'dp','ctx'}, dimensions={0} | all-to-all | bytes 1146880 | tf_op jit(solution)/shard_map/all_to_all | solution.py:255
  159.2 1.6 convolution_convert_fusion.7
  160.8 16.6 %all_to_all.49 = bf16[8,40,768]{2,1,0:T(8,128)(2,1)} all-to-all(bf16[8,40,768]{2,1,0:T(8,128)(2,1)S(1)} %bitcast.150), channel_id=1, replica_groups=mesh['dp'=4,'ctx'=2,'tensor'=4] {'dp','ctx'}, dimensions={0} | all-to-all | bytes 983040 | tf_op jit(solution)/shard_map/all_to_all | solution.py:255
  177.6 3.1 all-gather.3.cloned.1.call-done
  180.8 3.6 fusion.10
  184.3 1.8 copy-done.53
  186.2 3.8 convolution_convert_fusion.1
  190.0 1.5 add_reduce_fusion
  191.5 12.8 %all-gather.5.cloned.1.call-done = bf16[1280,768]{1,0:T(8,128)(2,1)} async-done(((bf16[320,768]{1,0:T(8,128)(2,1)}), bf16[1280,768]{1,0:T(8,128)(2,1)}) %all-gather.5.cloned.1.call-update) | async-done | bytes 1966096 | tf_op jit(solution)/shard_map/all_gather | solution.py:249
  204.3 6.7 %fusion.6 = bf16[1280,768]{1,0:T(8,128)(2,1)S(1)} fusion(f32[1280,768]{1,0:T(8,128)} %copy-done.53, bf16[1,768,768]{2,1,0:T(8,128)(2,1)S(1)} %copy-done, bf16[1280,768]{1,0:T(8,128)(2,1)} %all-gather.5.cloned.1.call-done, f32[1280]{0:T(1024)S(1)} %add_reduce_fusion), kind=kOutput, calls=%fused_computation.9 | convolution fusion | flops 1532559360 | bytes 9049088 | tf_op jit(solution)/shard_map/dot_general | solution.py:18
  211.0 1.3 copy-done.54
  212.4 3.0 convolution_convert_fusion
  215.4 22.7 %reduce-scatter.15.cloned.1.call-done = bf16[320,768]{1,0:T(8,128)(2,1)} async-done(((bf16[1280,768]{1,0:T(8,128)(2,1)}), bf16[320,768]{1,0:T(8,128)(2,1)}) %reduce-scatter.15.cloned.1.call-update) | async-done | bytes 491536 | tf_op jit(solution)/shard_map/reduce_scatter | solution.py:252
  238.1 5.5 all-to-all-start.1
  243.6 28.2 %reduce-scatter.17.cloned.1.call-done = bf16[320,768]{1,0:T(8,128)(2,1)} async-done(((bf16[1280,768]{1,0:T(8,128)(2,1)}), bf16[320,768]{1,0:T(8,128)(2,1)}) %reduce-scatter.17.cloned.1.call-update) | async-done | bytes 491536 | tf_op jit(solution)/shard_map/reduce_scatter | solution.py:252
  271.8 5.5 all-to-all-start.3
  277.4 1.7 fusion.37
  279.1 2.8 fusion.16
  281.9 9.2 %all-to-all-done.3 = bf16[8,40,768]{2,1,0:T(8,128)(2,1)} async-done(((bf16[8,40,768]{2,1,0:T(8,128)(2,1)}), bf16[8,40,768]{2,1,0:T(8,128)(2,1)}, u32[]{:S(2)}, u32[]{:S(2)}) %all-to-all-start.3) | async-done | bytes 491552 | tf_op jit(solution)/shard_map/all_to_all | solution.py:255
  291.2 2.5 convolution_convert_fusion.4
  294.5 2.8 fusion.12
  297.4 1.6 constant_dynamic-slice_fusion.1
  299.0 1.7 copy.132
  300.7 23.9 %reduce-scatter.27.cloned.1.call-done = bf16[128,1664]{1,0:T(8,128)(2,1)} async-done(((bf16[512,1664]{1,0:T(8,128)(2,1)}), bf16[128,1664]{1,0:T(8,128)(2,1)}) %reduce-scatter.27.cloned.1.call-update) | async-done | bytes 426000
  324.6 2.0 copy.129
  326.6 1.1 convert_element_type.176
  328.6 2.0 multiply_reduce_fusion
  330.8 8.5 %all_gather.40 = bf16[512,768]{0,1:T(8,128)(2,1)S(1)} all-gather(bf16[128,768]{0,1:T(8,128)(2,1)S(1)} %fusion.63), channel_id=1, replica_groups=mesh['dp'=4,'ctx'=2,'tensor'=4] {'tensor'}, dimensions={0}, use_global_device_ids=true | all-gather | bytes 983040 | tf_op jit(solution)/shard_map/all_gather | solution.py:249
  343.9 7.3 %attend_backward.1 = (bf16[512,192]{1,0:T(8,128)(2,1)S(1)}, bf16[1024,192]{1,0:T(8,128)(2,1)S(1)}, bf16[1024,192]{1,0:T(8,128)(2,1)S(1)}, f32[3,2,8,1024]{3,2,1,0:T(8,128)S(1)}) custom-call(s32[1]{0:T(128)} %bitcast.1.ctx_ref, s32[32]{0:T(128)S(1)} %copy-done.6, f32[32,3]{1,0:T(8,128)S(1)} %copy.108.table_ref, ...), custom_call_target="tpu_custom_call" | custom-call | tf_op jit(solution)/shard_map/attend_backward/pallas_call | solution.py:168
  352.6 1.2 maximum_bitcast_fusion
  354.7 1.1 convolution_convert_fusion.9
  355.9 5.4 fusion.13
  361.3 16.8 %reduce-scatter.19.cloned.1.call-done = bf16[1,512,384]{2,1,0:T(8,128)(2,1)} async-done(((bf16[1,1024,384]{2,1,0:T(8,128)(2,1)}), bf16[1,512,384]{2,1,0:T(8,128)(2,1)}) %reduce-scatter.19.cloned.1.call-update) | async-done | bytes 393232 | tf_op jit(solution)/shard_map/reduce_scatter | solution.py:370
  378.1 2.7 convolution_convert_fusion.3
  381.2 6.5 %convolution_bitcast_fusion = f32[1,768,768]{2,1,0:T(8,128)} fusion(bf16[1280,768]{1,0:T(8,128)(2,1)} %all-gather.5.cloned.1.call-done, f32[1280]{0:T(1024)S(1)} %copy-done.42, f32[1280,768]{1,0:T(8,128)} %copy-done.53), kind=kOutput, calls=%fused_computation.25 | convolution fusion | flops 1521745920 | bytes 8262656 | tf_op jit(solution)/shard_map/dot_general | solution.py:18
  388.7 36.2 %psum.15 = f32[32,3]{1,0:T(8,128)S(1)} all-reduce(f32[32,3]{1,0:T(8,128)S(1)} %select_reduce_fusion), channel_id=1, replica_groups=mesh['dp'=4,'ctx'=2,'tensor'=4] {'dp','ctx'}, use_global_device_ids=true, to_apply=%region_25.26 | all-reduce | flops 96 | bytes 768 | tf_op jit(solution)/shard_map/psum | solution.py:386
  425.7 18.1 %reduce-scatter.23.cloned.1.call-done = bf16[96,192]{1,0:T(8,128)(2,1)} async-done(((bf16[768,192]{1,0:T(8,128)(2,1)}), bf16[96,192]{1,0:T(8,128)(2,1)}) %reduce-scatter.23.cloned.1.call-update) | async-done | bytes 36880 | tf_op jit(solution)/shard_map/reduce_scatter | solution.py:221
  443.7 31.4 %all_gather.43 = bf16[768,192]{1,0:T(8,128)(2,1)S(1)} all-gather(bf16[96,192]{1,0:T(8,128)(2,1)} %reduce-scatter.23.cloned.1.call-done), channel_id=1, replica_groups=mesh['dp'=4,'ctx'=2,'tensor'=4] {'dp','ctx'}, dimensions={0}, use_global_device_ids=true | all-gather | bytes 331776 | tf_op jit(solution)/shard_map/all_gather | solution.py:222
  476.1 2.9 convolution_convert_fusion.2
  479.1 1.2 copy.131
  480.7 1.3 fusion.45
  482.0 8.6 %all_gather.41 = bf16[512,768]{0,1:T(8,128)(2,1)S(1)} all-gather(bf16[128,768]{0,1:T(8,128)(2,1)S(1)} %get-tuple-element.126), channel_id=1, replica_groups=mesh['dp'=4,'ctx'=2,'tensor'=4] {'tensor'}, dimensions={0}, use_global_device_ids=true | all-gather | bytes 983040 | tf_op jit(solution)/shard_map/all_gather | solution.py:249
  490.8 1.6 copy.118
  492.5 8.7 %all_gather.39 = bf16[512,768]{0,1:T(8,128)(2,1)S(1)} all-gather(bf16[128,768]{0,1:T(8,128)(2,1)S(1)} %get-tuple-element.127), channel_id=1, replica_groups=mesh['dp'=4,'ctx'=2,'tensor'=4] {'tensor'}, dimensions={0}, use_global_device_ids=true | all-gather | bytes 983040 | tf_op jit(solution)/shard_map/all_gather | solution.py:249
  501.2 1.2 copy.117
  502.4 37.3 %psum.14 = f32[10,768]{1,0:T(8,128)S(1)} all-reduce(f32[10,768]{1,0:T(8,128)S(1)} %maximum_bitcast_fusion.4), channel_id=1, replica_groups=mesh['dp'=4,'ctx'=2,'tensor'=4] {'dp','ctx','tensor'}, use_global_device_ids=true, to_apply=%region_21.22 | all-reduce | flops 7680 | bytes 61440 | tf_op jit(solution)/shard_map/psum | solution.py:382
  541.6 32.9 %all_gather.42 = bf16[768,576]{1,0:T(8,128)(2,1)S(1)} all-gather(bf16[96,576]{1,0:T(8,128)(2,1)} %reduce-scatter.21.cloned.1.call-done), channel_id=1, replica_groups=mesh['dp'=4,'ctx'=2,'tensor'=4] {'dp','ctx'}, dimensions={0}, use_global_device_ids=true | all-gather | bytes 995328 | tf_op jit(solution)/shard_map/all_gather | solution.py:222
  574.5 1.4 fusion.75
  575.9 2.2 copy.121
  578.1 2.2 copy.120
  (186 shorter events, 22.7 us)
Async XLA Ops:
  7.2 179.0 %copy-start = (bf16[1,768,768]{2,1,0:T(8,128)(2,1)S(1)}, bf16[1,768,768]{2,1,0:T(8,128)(2,1)}, u32[]{:S(2)}) copy-start(bf16[1,768,768]{2,1,0:T(8,128)(2,1)} %param.26) | copy-start | bytes 3538948
  7.2 36.9 %copy-start.21 = (bf16[1,512,768]{2,1,0:T(8,128)(2,1)S(1)}, bf16[1,512,768]{2,1,0:T(8,128)(2,1)}, u32[]{:S(2)}) copy-start(bf16[1,512,768]{2,1,0:T(8,128)(2,1)} %param.15) | copy-start | bytes 2359300
  7.2 36.9 %copy-start.38 = (f32[768]{0:T(1024)S(1)}, f32[768]{0:T(1024)}, u32[]{:S(2)}) copy-start(f32[768]{0:T(1024)} %param.16) | copy-start | bytes 9220
  7.2 114.6 %reduce-scatter.25.cloned.1.call-start = ((), (), s32[]{:S(2)}) async-start(), calls=%async_computation.19 | async-start | bytes 983040
  8.8 36.2 %copy-start.45 = (f32[512]{0:T(512)}, f32[512]{0:T(512)S(1)}, u32[]{:S(2)}) copy-start(f32[512]{0:T(512)S(1)} %add_rsqrt_fusion) | copy-start | bytes 6148
  44.1 0.9 copy-start.28
  44.1 1.2 copy-start.51
  44.1 1.3 copy-start.33
  76.6 15.1 %copy-start.18 = (bf16[768,192]{1,0:T(8,128)(2,1)}, bf16[768,192]{1,0:T(8,128)(2,1)S(1)}, u32[]{:S(2)}) copy-start(bf16[768,192]{1,0:T(8,128)(2,1)S(1)} %all_gather.35) | copy-start | bytes 884740
  91.7 3.8 copy-start.1
  93.0 87.7 %all-gather.3.cloned.1.call-start = ((), (), s32[]{:S(2)}) async-start(), calls=%async_computation.12 | async-start | bytes 2867200 | tf_op jit(solution)/shard_map/all_gather | solution.py:249
  95.5 28.7 %copy-start.30 = (f32[768]{0:T(1024)S(1)}, f32[768]{0:T(1024)}, u32[]{:S(2)}) copy-start(f32[768]{0:T(1024)} %param.23) | copy-start | bytes 9220
  97.3 37.2 %copy-start.32 = (bf16[768,8]{0,1:T(8,128)(2,1)S(1)}, bf16[768,8]{0,1:T(8,128)(2,1)}, u32[]{:S(2)}) copy-start(bf16[768,8]{0,1:T(8,128)(2,1)} %param.24) | copy-start | bytes 36868
  99.2 35.5 %copy-start.35 = (s32[1,512,2]{1,2,0:T(2,128)S(1)}, s32[1,512,2]{1,2,0:T(2,128)}, u32[]{:S(2)}) copy-start(s32[1,512,2]{1,2,0:T(2,128)} %param.27) | copy-start | bytes 12292
  122.9 207.7 %copy-start.14 = (bf16[128,768]{0,1:T(8,128)(2,1)}, bf16[128,768]{0,1:T(8,128)(2,1)S(1)}, u32[]{:S(2)}) copy-start(bf16[128,768]{0,1:T(8,128)(2,1)S(1)} %copy.127) | copy-start | bytes 589828
  124.1 206.5 %copy-start.43 = (f32[128]{0:T(128)}, f32[128]{0:T(128)S(1)}, u32[]{:S(2)}) copy-start(f32[128]{0:T(128)S(1)} %get-tuple-element.135) | copy-start | bytes 1540
  124.1 206.5 %copy-start.47 = (f32[128]{0:T(128)}, f32[128]{0:T(128)S(1)}, u32[]{:S(2)}) copy-start(f32[128]{0:T(128)S(1)} %get-tuple-element.134) | copy-start | bytes 1540
  125.3 9.3 %copy-start.26 = (bf16[128,768]{0,1:T(8,128)(2,1)}, bf16[128,768]{0,1:T(8,128)(2,1)S(1)}, u32[]{:S(2)}) copy-start(bf16[128,768]{0,1:T(8,128)(2,1)S(1)} %multiply_convert_fusion.5) | copy-start | bytes 589828
  133.6 0.9 copy-start.23
  159.1 45.2 %all-gather.5.cloned.1.call-start = ((), (), s32[]{:S(2)}) async-start(), calls=%async_computation.14 | async-start | bytes 2457600 | tf_op jit(solution)/shard_map/all_gather | solution.py:249
  177.4 60.7 %reduce-scatter.15.cloned.1.call-start = ((), (), s32[]{:S(2)}) async-start(), calls=%async_computation.13 | async-start | bytes 2457600 | tf_op jit(solution)/shard_map/reduce_scatter | solution.py:252
  184.3 1.9 copy-start.53
  190.0 81.8 %reduce-scatter.17.cloned.1.call-start = ((), (), s32[]{:S(2)}) async-start(), calls=%async_computation.15 | async-start | bytes 2457600 | tf_op jit(solution)/shard_map/reduce_scatter | solution.py:252
  191.5 19.5 %copy-start.41 = (f32[1280]{0:T(1024)}, f32[1280]{0:T(1024)S(1)}, u32[]{:S(2)}) copy-start(f32[1280]{0:T(1024)S(1)} %add_reduce_fusion) | copy-start | bytes 15364
  204.3 8.1 %copy-start.52 = (bf16[1,768,768]{2,1,0:T(8,128)(2,1)S(1)}, bf16[1,768,768]{2,1,0:T(8,128)(2,1)}, u32[]{:S(2)}) copy-start(bf16[1,768,768]{2,1,0:T(8,128)(2,1)} %param.25) | copy-start | bytes 3538948
  211.0 1.3 copy-start.54
  238.1 33.7 %all-to-all-start.1 = ((bf16[8,40,768]{2,1,0:T(8,128)(2,1)}), bf16[8,40,768]{2,1,0:T(8,128)(2,1)}, u32[]{:S(2)}, u32[]{:S(2)}) async-start(bf16[8,40,768]{2,1,0:T(8,128)(2,1)} %bitcast.149), calls=%async_computation.2 | async-start | bytes 983040 | tf_op jit(solution)/shard_map/all_to_all | solution.py:255
  271.8 19.4 %all-to-all-start.3 = ((bf16[8,40,768]{2,1,0:T(8,128)(2,1)}), bf16[8,40,768]{2,1,0:T(8,128)(2,1)}, u32[]{:S(2)}, u32[]{:S(2)}) async-start(bf16[8,40,768]{2,1,0:T(8,128)(2,1)} %bitcast.148), calls=%async_computation.5 | async-start | bytes 983040 | tf_op jit(solution)/shard_map/all_to_all | solution.py:255
  277.3 47.3 %reduce-scatter.27.cloned.1.call-start = ((), (), s32[]{:S(2)}) async-start(), calls=%async_computation.20 | async-start | bytes 2129920
  277.4 1.7 copy-start.34
  297.3 80.8 %reduce-scatter.19.cloned.1.call-start = ((), (), s32[]{:S(2)}) async-start(), calls=%async_computation.16 | async-start | bytes 1179648 | tf_op jit(solution)/shard_map/reduce_scatter | solution.py:370
  326.6 4.1 copy-start.10
  326.6 4.1 copy-start.24
  327.7 0.9 copy-start.20
  327.7 12.5 %copy-start.19 = (bf16[768,192]{1,0:T(8,128)(2,1)S(1)}, bf16[768,192]{1,0:T(8,128)(2,1)}, u32[]{:S(2)}) copy-start(bf16[768,192]{1,0:T(8,128)(2,1)} %copy-done.18) | copy-start | bytes 884740
  328.6 10.7 %copy-start.36 = (bf16[128,8]{0,1:T(8,128)(2,1)}, bf16[128,8]{0,1:T(8,128)(2,1)S(1)}, u32[]{:S(2)}) copy-start(bf16[128,8]{0,1:T(8,128)(2,1)S(1)} %select_reduce_fusion.4) | copy-start | bytes 6148
  330.6 8.7 %copy-start.16 = (f32[128,768]{0,1:T(8,128)}, f32[128,768]{0,1:T(8,128)S(1)}, u32[]{:S(2)}) copy-start(f32[128,768]{0,1:T(8,128)S(1)} %get-tuple-element.136) | copy-start | bytes 1179652
  330.6 8.7 %copy-start.49 = (f32[128]{0:T(128)}, f32[128]{0:T(128)S(1)}, u32[]{:S(2)}) copy-start(f32[128]{0:T(128)S(1)} %broadcast_multiply_fusion.1) | copy-start | bytes 1540
  339.3 0.9 copy-start.12
  342.3 1.0 copy-start.2
  351.9 0.7 copy-start.8
  352.6 1.3 copy-start.7
  352.6 1.4 copy-start.46
  352.6 2.1 copy-start.13
  353.8 89.9 %reduce-scatter.23.cloned.1.call-start = ((), (), s32[]{:S(2)}) async-start(), calls=%async_computation.18 | async-start | bytes 442368 | tf_op jit(solution)/shard_map/reduce_scatter | solution.py:221
  355.8 22.3 %copy-start.9 = (bf16[512,192]{1,0:T(8,128)(2,1)S(1)}, bf16[512,192]{1,0:T(8,128)(2,1)}, u32[]{:S(2)}) copy-start(bf16[512,192]{1,0:T(8,128)(2,1)} %copy-done.8) | copy-start | bytes 589828
  355.9 22.3 %copy-start.29 = (bf16[768,576]{1,0:T(8,128)(2,1)S(1)}, bf16[768,576]{1,0:T(8,128)(2,1)}, u32[]{:S(2)}) copy-start(bf16[768,576]{1,0:T(8,128)(2,1)} %copy-done.28) | copy-start | bytes 2654212
  355.9 123.2 %reduce-scatter.29.cloned.1.call-start = ((), (), s32[]{:S(2)}) async-start(), calls=%async_computation.21 | async-start | bytes 983040
  361.3 19.9 %copy-start.42 = (f32[1280]{0:T(1024)S(1)}, f32[1280]{0:T(1024)}, u32[]{:S(2)}) copy-start(f32[1280]{0:T(1024)} %copy-done.41) | copy-start | bytes 15364
  380.9 6.9 %copy-start.40 = (f32[768]{0:T(1024)S(1)}, f32[768]{0:T(1024)}, u32[]{:S(2)}) copy-start(f32[768]{0:T(1024)} %get-tuple-element.110) | copy-start | bytes 9220
  380.9 6.9 %copy-start.4 = (f32[3,2,8,1024]{3,2,1,0:T(8,128)S(1)}, f32[3,2,8,1024]{3,2,1,0:T(8,128)}, u32[]{:S(2)}) copy-start(f32[3,2,8,1024]{3,2,1,0:T(8,128)} %copy-done.3) | copy-start | bytes 589828
  380.9 44.6 %copy-start.27 = (bf16[128,768]{0,1:T(8,128)(2,1)S(1)}, bf16[128,768]{0,1:T(8,128)(2,1)}, u32[]{:S(2)}) copy-start(bf16[128,768]{0,1:T(8,128)(2,1)} %copy-done.26) | copy-start | bytes 589828
  380.9 44.6 %copy-start.37 = (bf16[128,8]{0,1:T(8,128)(2,1)S(1)}, bf16[128,8]{0,1:T(8,128)(2,1)}, u32[]{:S(2)}) copy-start(bf16[128,8]{0,1:T(8,128)(2,1)} %copy-done.36) | copy-start | bytes 6148
  380.9 160.7 %reduce-scatter.21.cloned.1.call-start = ((), (), s32[]{:S(2)}) async-start(), calls=%async_computation.17 | async-start | bytes 1105920 | tf_op jit(solution)/shard_map/reduce_scatter | solution.py:221
  387.7 88.3 %copy-start.22 = (bf16[1,512,768]{2,1,0:T(8,128)(2,1)S(1)}, bf16[1,512,768]{2,1,0:T(8,128)(2,1)}, u32[]{:S(2)}) copy-start(bf16[1,512,768]{2,1,0:T(8,128)(2,1)} %param.15) | copy-start | bytes 2359300
  387.7 88.3 %copy-start.39 = (f32[768]{0:T(1024)S(1)}, f32[768]{0:T(1024)}, u32[]{:S(2)}) copy-start(f32[768]{0:T(1024)} %param.16) | copy-start | bytes 9220
  476.1 4.2 copy-start.11
  479.0 1.6 copy-start.15
  479.0 1.6 copy-start.17
  479.0 1.6 copy-start.25
  479.0 1.6 copy-start.31
  479.0 1.6 copy-start.44
  479.1 1.6 copy-start.48
  479.1 1.6 copy-start.50
  (3 other events, 2.0 us)
Sparse Core Ops, SparseCore 0:
  93.2 28.6 reduce-scatter.24
  159.3 21.4 all-gather.2
  182.4 21.8 all-gather.4
  207.5 30.6 reduce-scatter.14
  241.1 30.6 reduce-scatter.16
  297.4 27.1 reduce-scatter.26
  353.9 24.1 reduce-scatter.18
  382.3 61.3 reduce-scatter.22
  447.0 22.2 reduce-scatter.28
  479.2 62.2 reduce-scatter.20
